TPU v7x, 32 devices: a whole 2x2x4 slice. The times are simulated.
32 devices in a mesh: grp: 2 (over y), ha: 4 (over z), wa: 4 (over x, core).
Axes of the slice: x: 2, y: 2, z: 4, core: 2. Of those that a mesh axis runs over, the one named last changes fastest.
Arguments:
- inputs: bfloat16 [8, 16, 64, 128], P('grp', 'ha', 'wa'), parts along dimension 0, may hold values from -40 to 40
- upstream: bfloat16 [8, 16, 64, 128], P('grp', 'ha', 'wa'), parts along dimension 0, may hold values from -40 to 40
- kernels: bfloat16 [4, 3456, 128], replicated, may hold values from -0.109375 to 0.109375
- norm_gain: float32 [4, 128], replicated, may hold values from 0.1 to 1.9
- norm_shift: float32 [4, 128], replicated, may hold values from -3 to 3
Outputs:
- input_grad: bfloat16 [8, 16, 64, 128], P('grp', 'ha', 'wa'), parts along dimension 0
- kernel_grads: float32 [8, 27, 16384], P('grp', None, ('ha', 'wa')), parts along dimension 0
- norm_grads: float32 [4, 4, 128], P('grp'), parts along dimension 0
There are 2 independent parts, one for each index of `grp`. A program takes and returns all parts, laid end to end along the dimension named above; an argument that names none is the same for every part. Nothing has to cross between parts.
All inputs are finite; a program needn't handle non-finite values.
Results may differ from a plain program's by a relative error of at most 0.0059.
Values may be sent and summed in bfloat16 or wider, within the bound.
A program may use at most 64 MiB of HBM per device.

v0:
```python
import math

import jax
import jax.numpy as jnp
from jax import lax
from jax.experimental import pallas as pl
from jax.experimental.pallas import tpu as pltpu
from jax.sharding import PartitionSpec as P

norm_eps = 1e-06
MESH = pl.DeviceIdType.MESH


def exchange_kernel(stat, edges, all_stat, border, stat_send, stat_recv, edge_send, edge_recv, *, rows_n, cols_n, pieces):
    n = rows_n * cols_n
    g, a, w = lax.axis_index("grp"), lax.axis_index("ha"), lax.axis_index("wa")
    me = a * cols_n + w
    border[...] = jnp.zeros_like(border)
    barrier = pltpu.get_barrier_semaphore()

    def device(index):
        return (g, lax.div(index, cols_n), lax.rem(index, cols_n))

    for k in range(1, n):
        pl.semaphore_signal(barrier, inc=1, device_id=device(lax.rem(me + k, n)), device_id_type=MESH)
    pl.semaphore_wait(barrier, n - 1)
    plans = []
    for i, (dh, dw, src, dst, size) in enumerate(pieces):
        ok_to = (a + dh >= 0) & (a + dh < rows_n) & (w + dw >= 0) & (w + dw < cols_n)
        ok_from = (a - dh >= 0) & (a - dh < rows_n) & (w - dw >= 0) & (w - dw < cols_n)
        copy = pltpu.make_async_remote_copy(
            edges.at[pl.ds(src, size)],
            border.at[pl.ds(dst, size)],
            edge_send.at[i],
            edge_recv.at[i],
            device_id=(g, a + dh, w + dw),
            device_id_type=MESH,
        )
        plans.append((ok_to, ok_from, copy))

        @pl.when(ok_to)
        def _():
            copy.start()

    all_stat[0] = stat[...]
    copies = []
    for k in range(1, n):
        copy = pltpu.make_async_remote_copy(
            stat,
            all_stat.at[k],
            stat_send.at[k],
            stat_recv.at[k],
            device_id=device(lax.rem(me + k, n)),
            device_id_type=MESH,
        )
        copy.start()
        copies.append(copy)
    for copy in copies:
        copy.wait()
    for ok_to, ok_from, copy in plans:

        @pl.when(ok_to)
        def _():
            copy.wait_send()

        @pl.when(ok_from)
        def _():
            copy.wait_recv()


def border_plan(frames, rows, width):
    moves = [(-1, 0, frames * width), (1, 0, frames * width), (0, -1, frames * rows), (0, 1, frames * rows)]
    moves += [(dh, dw, 8 * pl.cdiv(frames, 8)) for dh in (-1, 1) for dw in (-1, 1)]
    plan, offset = {}, 0
    for dh, dw, size in moves:
        plan[dh, dw] = (offset, size)
        offset += size
    return plan, offset


def exchange(stat, packed, plan, rows_n, cols_n):
    pieces = [(dh, dw, start, start, size) for (dh, dw), (start, size) in plan.items()]
    n = rows_n * cols_n
    vmem = pl.BlockSpec(memory_space=pltpu.VMEM)

    def run(*args):
        return exchange_kernel(*args, rows_n=rows_n, cols_n=cols_n, pieces=pieces)

    return pl.pallas_call(
        run,
        out_shape=(
            jax.ShapeDtypeStruct((n,) + stat.shape, jnp.float32),
            jax.ShapeDtypeStruct(packed.shape, jnp.float32),
        ),
        in_specs=[vmem, vmem],
        out_specs=(vmem, vmem),
        scratch_shapes=[
            pltpu.SemaphoreType.DMA((n,)),
            pltpu.SemaphoreType.DMA((n,)),
            pltpu.SemaphoreType.DMA((8,)),
            pltpu.SemaphoreType.DMA((8,)),
        ],
        compiler_params=pltpu.CompilerParams(collective_id=0, has_side_effects=True),
    )(stat, packed)


def pack(edges, values, plan):
    frames, rows, width, chans = values.shape
    for (dh, dw), (start, size) in plan.items():
        row = 0 if dh < 0 else rows - 1
        col = 0 if dw < 0 else width - 1
        for f in range(frames):
            if dw == 0:
                edges[pl.ds(start + f * width, width), :] = values[f, row]
            elif dh == 0:
                for r in range(rows):
                    edges[pl.ds(start + f * rows + r, 1), :] = values[f, r, pl.ds(col, 1), :]
            else:
                edges[pl.ds(start + f, 1), :] = values[f, row, pl.ds(col, 1), :]
        if dh != 0 and dw != 0 and size > frames:
            edges[pl.ds(start + frames, size - frames), :] = jnp.zeros((size - frames, chans), jnp.float32)


def unpack(wide, values, border, plan):
    frames, rows, width, chans = values.shape
    wide[...] = jnp.zeros_like(wide)
    wide[:, 1 : rows + 1, 8 : 8 + width, :] = values[...]
    for (dh, dw), (start, size) in plan.items():
        row = rows + 1 if dh < 0 else 0
        col = 8 + width if dw < 0 else 7
        for f in range(frames):
            if dw == 0:
                wide[f, row, 8 : 8 + width, :] = border[pl.ds(start + f * width, width), :]
            elif dh == 0:
                for r in range(rows):
                    wide[f, r + 1, pl.ds(col, 1), :] = border[pl.ds(start + f * rows + r, 1), :]
            else:
                wide[f, row, pl.ds(col, 1), :] = border[pl.ds(start + f, 1), :]


def fill_patches(patches, shifted, wide, width, lead, tail):
    frames, rows_wide, _, chans = wide.shape
    rows = rows_wide - 2
    for e in range(3):
        shifted[e, lead[0] : lead[0] + frames] = wide[:, :, 7 + e : 7 + e + width, :].astype(jnp.bfloat16)
        for f in range(lead[0]):
            if lead[1]:
                shifted[e, f] = wide[0, :, 7 + e : 7 + e + width, :].astype(jnp.bfloat16)
            else:
                shifted[e, f] = jnp.zeros((rows_wide, width, chans), jnp.bfloat16)
        for f in range(tail):
            shifted[e, lead[0] + frames + f] = jnp.zeros((rows_wide, width, chans), jnp.bfloat16)
    count = lead[0] + frames + tail - 2
    for tap in range(27):
        t, b, e = tap // 9, tap // 3 % 3, tap % 3
        piece = shifted[e, t : t + count, b : b + rows]
        patches[:, tap * chans : (tap + 1) * chans] = piece.reshape(count * rows * width, chans)


def total_mean(x, count):
    return jnp.sum(x, axis=1, keepdims=True) / count


def forward_kernel(values, border, all_stat, mask, kernel, gain, shift, *rest, plan, count, add, conv):
    rest = list(rest)
    base = rest.pop(0) if add else None
    normed, scale_out, patches = rest[:3]
    rest = rest[3:]
    if conv:
        result, stat, edges = rest[:3]
        rest = rest[3:]
    wide, shifted = rest
    frames, rows, width, chans = values.shape
    local = rows * width
    unpack(wide, values, border, plan)
    all_sums, all_squares = all_stat[:, :frames], all_stat[:, frames:]
    mean = total_mean(jnp.sum(all_sums, axis=0), count)
    gap = all_sums * (1.0 / local) - mean[None]
    var = total_mean(jnp.sum(all_squares + local * gap * gap, axis=0), count)
    inv_std = lax.rsqrt(var + norm_eps)
    scale_out[...] = jnp.broadcast_to(inv_std, (frames, chans))
    for f in range(frames):
        x = (wide[f] - mean[f : f + 1][None]) * inv_std[f : f + 1][None]
        normed[f] = x
        pre = x * gain[...][None] + shift[...][None]
        wide[f] = pre * jax.nn.sigmoid(pre) * mask[...]
    fill_patches(patches, shifted, wide, width, (2, True), 0)
    if not conv:
        return
    out = jnp.dot(patches[...], kernel[...], preferred_element_type=jnp.float32).reshape(frames, rows, width, chans)
    if add:
        out = out + base[...]
    result[...] = out
    fill_stat(stat, out)
    pack(edges, result, plan)


def fill_stat(stat, out):
    frames, rows, width, _ = out.shape
    sums = jnp.sum(out, axis=(1, 2))
    stat[:frames] = sums
    centred = out - (sums * (1.0 / (rows * width)))[:, None, None]
    stat[frames:] = jnp.sum(centred * centred, axis=(1, 2))


def start_kernel(inputs, upstream, values, up, stat, edges, up_edges, *, plan):
    values[...] = inputs[...].astype(jnp.float32)
    up[...] = upstream[...].astype(jnp.float32)
    fill_stat(stat, values[...])
    pack(edges, values, plan)
    pack(up_edges, up, plan)


def backward_kernel(*refs, plan, count, normed_in, add):
    refs = list(refs)
    values, border, all_stat, mask, kernel, gain, shift, normed, patches = refs[:9]
    refs = refs[9:]
    if normed_in:
        last_normed, last_inv, last_gain = refs[:3]
        refs = refs[3:]
    base = refs.pop(0) if add else None
    keep, term, dn_out, stat, edges, wide, shifted, out_patches = refs
    frames, rows, width, chans = values.shape
    unpack(wide, values, border, plan)
    if normed_in:
        total = jnp.sum(all_stat[...], axis=0)
        s1 = total_mean(total[:frames] * last_gain[...], count)
        s2 = total_mean(total[frames:] * last_gain[...], count)
        for f in range(frames):
            into = last_inv[f : f + 1][None] * (
                wide[f] * last_gain[...][None] - s1[f : f + 1][None] - last_normed[f] * s2[f : f + 1][None]
            )
            into = into * mask[...]
            if add:
                into = into + base[f]
            wide[f] = into
    keep[...] = wide[...]
    flat = wide[:, 1 : rows + 1, 8 : 8 + width, :].astype(jnp.bfloat16).reshape(frames * rows * width, chans)
    term[...] = lax.dot_general(patches[...], flat, (((0,), (0,)), ((), ())), preferred_element_type=jnp.float32)
    fill_patches(out_patches, shifted, wide, width, (2, False), 2)
    back = jnp.zeros(((frames + 2) * rows * width, chans), jnp.float32)
    for tap in range(27):
        back = back + lax.dot_general(
            out_patches[:, tap * chans : (tap + 1) * chans],
            kernel[(26 - tap) * chans : (27 - tap) * chans, :],
            (((1,), (1,)), ((), ())),
            preferred_element_type=jnp.float32,
        )
    back = back.reshape(frames + 2, rows, width, chans)
    for f in range(frames):
        grad = back[0] + back[1] + back[2] if f == 0 else back[f + 2]
        x = normed[f, 1 : rows + 1, 8 : 8 + width, :]
        pre = x * gain[...][None] + shift[...][None]
        sig = jax.nn.sigmoid(pre)
        dn = grad * (sig * (1.0 + pre * (1.0 - sig)))
        dn_out[f] = dn
        stat[f : f + 1] = jnp.sum(dn, axis=(0, 1))[None]
        stat[frames + f : frames + f + 1] = jnp.sum(dn * x, axis=(0, 1))[None]
    pack(edges, dn_out, plan)


def call(body, args, outs, scratch):
    vmem = pl.BlockSpec(memory_space=pltpu.VMEM)
    return pl.pallas_call(
        body,
        out_shape=tuple(jax.ShapeDtypeStruct(shape, dtype) for shape, dtype in outs),
        in_specs=[vmem] * len(args),
        out_specs=(vmem,) * len(outs),
        scratch_shapes=[pltpu.VMEM(shape, dtype) for shape, dtype in scratch],
        compiler_params=pltpu.CompilerParams(vmem_limit_bytes=40 * 2**20),
    )(*args)


def body(inputs, upstream, kernels, norm_gain, norm_shift):
    frames, rows, width, chans = inputs.shape
    rows_n, cols_n = lax.axis_size("ha"), lax.axis_size("wa")
    total_rows, total_width = rows * rows_n, width * cols_n
    count = total_rows * total_width * chans
    scale = 1.0 / math.sqrt(frames * total_rows * total_width)
    layers = kernels.shape[0]
    a, w = lax.axis_index("ha"), lax.axis_index("wa")
    row_id = a * rows - 1 + jnp.arange(rows + 2)
    col_id = w * width - 8 + jnp.arange(width + 16)
    inside = ((row_id >= 0) & (row_id < total_rows))[:, None] & ((col_id >= 0) & (col_id < total_width))[None]
    mask = jnp.broadcast_to(inside[:, :, None].astype(jnp.float32), (rows + 2, width + 16, chans))
    plan, edge_rows = border_plan(frames, rows, width)
    f32, bf16 = jnp.float32, jnp.bfloat16
    own = ((frames, rows, width, chans), f32)
    stat_t = ((2 * frames, chans), f32)
    edge_t = ((edge_rows, chans), f32)
    wide_t = ((frames, rows + 2, width + 16, chans), f32)
    inv_t = ((frames, chans), f32)
    patch_t = ((frames * rows * width, 27 * chans), bf16)
    gains = [norm_gain[j : j + 1] for j in range(layers)]
    shifts = [norm_shift[j : j + 1] for j in range(layers)]

    values, up, stat, edges, up_edges = call(
        lambda *r: start_kernel(*r, plan=plan), [inputs, upstream], [own, own, stat_t, edge_t, edge_t], []
    )
    stream = values
    saved = []
    for layer in range(layers):
        all_stat, border = exchange(stat, edges, plan, rows_n, cols_n)
        add = layer % 2 == 1 and layer < layers - 1
        conv = layer < layers - 1
        args = [values, border, all_stat, mask, kernels[layer], gains[layer], shifts[layer]]
        if add:
            args.append(stream)
        outs = [wide_t, inv_t, patch_t] + ([own, stat_t, edge_t] if conv else [])

        def run(*r, add=add, conv=conv):
            forward_kernel(*r, plan=plan, count=count, add=add, conv=conv)

        got = call(run, args, outs, [wide_t, ((3, frames + 2, rows + 2, width, chans), bf16)])
        saved.append(got[:3])
        if conv:
            values, stat, edges = got[3:]
            if add:
                stream = values

    terms, gain_sums, shift_sums = [None] * layers, [None] * layers, [None] * layers
    values, edges, stat = up, up_edges, jnp.zeros(stat_t[0], f32)
    grad_stream = None
    for layer in range(layers - 1, -1, -1):
        all_stat, border = exchange(stat, edges, plan, rows_n, cols_n)
        args = [values, border, all_stat, mask, kernels[layer], gains[layer], shifts[layer], saved[layer][0], saved[layer][2]]
        normed_in = layer < layers - 1
        add = normed_in and layer % 2 == 1
        if normed_in:
            args += [saved[layer + 1][0], saved[layer + 1][1], gains[layer + 1]]
            total = jnp.sum(all_stat, axis=0)
            shift_sums[layer + 1] = jnp.sum(total[:frames], axis=0)
            gain_sums[layer + 1] = jnp.sum(total[frames:], axis=0)
        if add:
            args.append(grad_stream)

        def run_back(*r, normed_in=normed_in, add=add):
            backward_kernel(*r, plan=plan, count=count, normed_in=normed_in, add=add)

        keep, term, values, stat, edges = call(
            run_back,
            args,
            [wide_t, ((27 * chans, chans), f32), own, stat_t, edge_t],
            [
                wide_t,
                ((3, frames + 4, rows + 2, width, chans), bf16),
                (((frames + 2) * rows * width, 27 * chans), bf16),
            ],
        )
        if layer % 2 == 1:
            grad_stream = keep
        share = lax.psum_scatter(term.reshape(27, chans, chans), ("ha", "wa"), scatter_dimension=1, tiled=True)
        terms[layer] = share.reshape(27, -1)
    all_stat, _ = exchange(stat, edges, plan, rows_n, cols_n)
    total = jnp.sum(all_stat, axis=0)
    shift_sums[0] = jnp.sum(total[:frames], axis=0)
    gain_sums[0] = jnp.sum(total[frames:], axis=0)
    s1 = (jnp.sum(total[:frames] * norm_gain[0], axis=1) / count)[:, None, None, None]
    s2 = (jnp.sum(total[frames:] * norm_gain[0], axis=1) / count)[:, None, None, None]
    cut = (slice(None), slice(1, rows + 1), slice(8, 8 + width))
    into = saved[0][1][:, None, None] * (values * norm_gain[0] - s1 - saved[0][0][cut] * s2)
    input_grad = (grad_stream[cut] + into).astype(jnp.bfloat16)
    norm_grads = jnp.stack([jnp.stack(gain_sums), jnp.stack(shift_sums)]) * scale
    return (input_grad, jnp.stack(terms) * scale, norm_grads)


def solution(mesh):
    return jax.shard_map(
        body,
        mesh=mesh,
        in_specs=(P("grp", "ha", "wa", None), P("grp", "ha", "wa", None), P(), P(), P()),
        out_specs=(P("grp", "ha", "wa", None), P("grp", None, ("ha", "wa")), P("grp", None, None)),
        check_vma=False,
    )
```

profile of v0, /device:TPU:0, one launch (start us, length us, event | category | flops | bytes accessed | tf_op | source)
XLA Modules:
  0.0 368.4 jit_solution(4823304732145280845)
XLA Ops:
  7.3 2.3 slice_bitcast_fusion
  14.7 11.6 %shard_map.77 = (f32[16,8,128]{2,1,0:T(8,128)}, f32[192,128]{1,0:T(8,128)}) custom-call(f32[8,128]{1,0:T(8,128)} %broadcast_in_dim.4.args_0_, f32[192,128]{1,0:T(8,128)} %copy-done.61), custom_call_target="tpu_custom_call" | custom-call | tf_op jit(solution)/shard_map/pallas_call | solution.py:89
  26.3 9.3 %shard_map.78 = (f32[16,8,128]{2,1,0:T(8,128)}, f32[192,128]{1,0:T(8,128)}) custom-call(f32[8,128]{1,0:T(8,128)} %copy-done.85, f32[192,128]{1,0:T(8,128)} %copy-done.57), custom_call_target="tpu_custom_call" | custom-call | tf_op jit(solution)/shard_map/pallas_call | solution.py:89
  41.3 1.2 copy-done.11
  45.7 9.6 %shard_map.80 = (f32[16,8,128]{2,1,0:T(8,128)}, f32[192,128]{1,0:T(8,128)}) custom-call(f32[8,128]{1,0:T(8,128)} %copy-done.88, f32[192,128]{1,0:T(8,128)} %copy-done.60), custom_call_target="tpu_custom_call" | custom-call | tf_op jit(solution)/shard_map/pallas_call | solution.py:89
  61.3 1.2 copy-done.9
  65.8 9.6 %shard_map.82 = (f32[16,8,128]{2,1,0:T(8,128)}, f32[192,128]{1,0:T(8,128)}) custom-call(f32[8,128]{1,0:T(8,128)} %copy-done.86, f32[192,128]{1,0:T(8,128)} %copy-done.58), custom_call_target="tpu_custom_call" | custom-call | tf_op jit(solution)/shard_map/pallas_call | solution.py:89
  85.0 9.6 %shard_map.84 = (f32[16,8,128]{2,1,0:T(8,128)}, f32[192,128]{1,0:T(8,128)}) custom-call(f32[8,128]{1,0:T(8,128)} %copy-done.87, f32[192,128]{1,0:T(8,128)} %copy-done.59), custom_call_target="tpu_custom_call" | custom-call | tf_op jit(solution)/shard_map/pallas_call | solution.py:89
  104.2 1.4 shard_map.86
  109.6 9.7 %shard_map.87 = (f32[16,8,128]{2,1,0:T(8,128)}, f32[192,128]{1,0:T(8,128)}) custom-call(f32[8,128]{1,0:T(8,128)} %copy-done.84, f32[192,128]{1,0:T(8,128)} %copy-done.56), custom_call_target="tpu_custom_call" | custom-call | tf_op jit(solution)/shard_map/pallas_call | solution.py:89
  119.3 1.5 copy-done.14
  124.7 1.8 shard_map.88
  129.9 9.6 %shard_map.89 = (f32[16,8,128]{2,1,0:T(8,128)}, f32[192,128]{1,0:T(8,128)}) custom-call(f32[8,128]{1,0:T(8,128)} %copy-done.83, f32[192,128]{1,0:T(8,128)} %copy-done.55), custom_call_target="tpu_custom_call" | custom-call | tf_op jit(solution)/shard_map/pallas_call | solution.py:89
  139.6 1.5 copy-done.10
  142.8 1.5 shard_map.90
  144.4 1.2 copy-done.8
  148.4 9.7 %shard_map.91 = (f32[16,8,128]{2,1,0:T(8,128)}, f32[192,128]{1,0:T(8,128)}) custom-call(f32[8,128]{1,0:T(8,128)} %copy-done.82, f32[192,128]{1,0:T(8,128)} %copy-done.54), custom_call_target="tpu_custom_call" | custom-call | tf_op jit(solution)/shard_map/pallas_call | solution.py:89
  161.8 2.6 shard_map.92
  166.6 9.6 %shard_map.93 = (f32[16,8,128]{2,1,0:T(8,128)}, f32[192,128]{1,0:T(8,128)}) custom-call(f32[8,128]{1,0:T(8,128)} %copy-done.81, f32[192,128]{1,0:T(8,128)} %copy-done.53), custom_call_target="tpu_custom_call" | custom-call | tf_op jit(solution)/shard_map/pallas_call | solution.py:89
  177.9 1.7 add_convert_fusion
  179.6 54.2 %reduce-scatter.9.cloned.1.call-done = f32[27,8,128]{2,1,0:T(8,128)} async-done(((f32[27,128,128]{2,1,0:T(8,128)}), f32[27,8,128]{2,1,0:T(8,128)}) %reduce-scatter.9.cloned.1.call-update) | async-done | bytes 110608 | tf_op jit(solution)/shard_map/reduce_scatter | solution.py:352
  233.8 63.0 %reduce-scatter.7.cloned.1.call-done = f32[27,8,128]{2,1,0:T(8,128)} async-done(((f32[27,128,128]{2,1,0:T(8,128)}), f32[27,8,128]{2,1,0:T(8,128)}) %reduce-scatter.7.cloned.1.call-update) | async-done | bytes 110608 | tf_op jit(solution)/shard_map/reduce_scatter | solution.py:352
  296.8 62.8 %reduce-scatter.5.cloned.1.call-done = f32[27,8,128]{2,1,0:T(8,128)} async-done(((f32[27,128,128]{2,1,0:T(8,128)}), f32[27,8,128]{2,1,0:T(8,128)}) %reduce-scatter.5.cloned.1.call-update) | async-done | bytes 110608 | tf_op jit(solution)/shard_map/reduce_scatter | solution.py:352
  359.6 2.2 maximum_multiply_fusion
  (228 shorter events, 65.5 us)
Async XLA Ops:
  7.2 172.5 %reduce-scatter.11.cloned.1.call-start = ((), (), s32[]{:S(2)}) async-start(), calls=%async_computation.7 | async-start | bytes 1880064 | tf_op jit(solution)/shard_map/reduce_scatter | solution.py:352
  7.2 3.0 copy-start.98
  7.3 3.0 copy-start.99
  7.3 3.6 copy-start.70
  7.3 3.5 copy-start.71
  99.9 5.7 %copy-start.19 = (f32[4,6,32,128]{3,2,1,0:T(8,128)}, f32[4,6,32,128]{3,2,1,0:T(8,128)S(1)}, u32[]{:S(2)}) copy-start(f32[4,6,32,128]{3,2,1,0:T(8,128)S(1)} %get-tuple-element.88.r_7_.r_9_) | copy-start | bytes 1179652
  109.5 9.8 %copy-start.5 = (f32[6,32,128]{2,1,0:T(8,128)S(1)}, f32[6,32,128]{2,1,0:T(8,128)}, u32[]{:S(2)}) copy-start(f32[6,32,128]{2,1,0:T(8,128)} %copy-done) | copy-start | bytes 294916
  109.5 9.8 %copy-start.18 = (f32[4,6,32,128]{3,2,1,0:T(8,128)S(1)}, f32[4,6,32,128]{3,2,1,0:T(8,128)}, u32[]{:S(2)}) copy-start(f32[4,6,32,128]{3,2,1,0:T(8,128)} %copy-done.17) | copy-start | bytes 1179652
  109.5 9.8 %copy-start.20 = (f32[4,6,32,128]{3,2,1,0:T(8,128)S(1)}, f32[4,6,32,128]{3,2,1,0:T(8,128)}, u32[]{:S(2)}) copy-start(f32[4,6,32,128]{3,2,1,0:T(8,128)} %copy-done.19) | copy-start | bytes 1179652
  109.5 124.3 %reduce-scatter.9.cloned.1.call-start = ((), (), s32[]{:S(2)}) async-start(), calls=%async_computation.6 | async-start | bytes 1880064 | tf_op jit(solution)/shard_map/reduce_scatter | solution.py:352
  119.3 1.5 copy-start.14
  129.6 9.9 %copy-start.16 = (f32[4,6,32,128]{3,2,1,0:T(8,128)S(1)}, f32[4,6,32,128]{3,2,1,0:T(8,128)}, u32[]{:S(2)}) copy-start(f32[4,6,32,128]{3,2,1,0:T(8,128)} %copy-done.15) | copy-start | bytes 1179652
  129.7 9.9 %copy-start.27 = (f32[4,6,32,128]{3,2,1,0:T(8,128)S(1)}, f32[4,6,32,128]{3,2,1,0:T(8,128)}, u32[]{:S(2)}) copy-start(f32[4,6,32,128]{3,2,1,0:T(8,128)} %copy-done.26) | copy-start | bytes 1179652
  129.7 9.9 %copy-start.76 = (f32[1,128]{1,0:T(1,128)S(1)}, f32[1,128]{1,0:T(1,128)}, u32[]{:S(2)}) copy-start(f32[1,128]{1,0:T(1,128)} %get-tuple-element.150.r_6_) | copy-start | bytes 1540
  129.7 9.9 %copy-start.94 = (f32[4,128]{1,0:T(4,128)S(1)}, f32[4,128]{1,0:T(4,128)}, u32[]{:S(2)}) copy-start(f32[4,128]{1,0:T(4,128)} %copy-done.93) | copy-start | bytes 6148
  129.7 9.9 %copy-start.39 = (f32[4,4,16,128]{3,2,1,0:T(8,128)S(1)}, f32[4,4,16,128]{3,2,1,0:T(8,128)}, u32[]{:S(2)}) copy-start(f32[4,4,16,128]{3,2,1,0:T(8,128)} %copy-done.38) | copy-start | bytes 393220
  129.7 167.1 %reduce-scatter.7.cloned.1.call-start = ((), (), s32[]{:S(2)}) async-start(), calls=%async_computation.5 | async-start | bytes 1880064 | tf_op jit(solution)/shard_map/reduce_scatter | solution.py:352
  139.6 1.5 copy-start.10
  148.3 9.8 %copy-start.12 = (bf16[256,3456]{1,0:T(8,128)(2,1)S(1)}, bf16[256,3456]{1,0:T(8,128)(2,1)}, u32[]{:S(2)}) copy-start(bf16[256,3456]{1,0:T(8,128)(2,1)} %copy-done.11) | copy-start | bytes 5308420
  148.3 9.8 %copy-start.74 = (f32[1,128]{1,0:T(1,128)S(1)}, f32[1,128]{1,0:T(1,128)}, u32[]{:S(2)}) copy-start(f32[1,128]{1,0:T(1,128)} %get-tuple-element.152.r_6_) | copy-start | bytes 1540
  148.3 9.8 %copy-start.92 = (f32[4,128]{1,0:T(4,128)S(1)}, f32[4,128]{1,0:T(4,128)}, u32[]{:S(2)}) copy-start(f32[4,128]{1,0:T(4,128)} %copy-done.91) | copy-start | bytes 6148
  148.3 211.3 %reduce-scatter.5.cloned.1.call-start = ((), (), s32[]{:S(2)}) async-start(), calls=%async_computation.4 | async-start | bytes 1880064 | tf_op jit(solution)/shard_map/reduce_scatter | solution.py:352
  165.7 11.5 %copy-start.97 = (f32[128]{0:T(128)S(1)}, f32[128]{0:T(128)}, u32[]{:S(2)}) copy-start(f32[128]{0:T(128)} %get-tuple-element.141) | copy-start | bytes 1540
  165.7 12.3 %copy-start.90 = (f32[4,128]{1,0:T(4,128)S(1)}, f32[4,128]{1,0:T(4,128)}, u32[]{:S(2)}) copy-start(f32[4,128]{1,0:T(4,128)} %copy-done.89) | copy-start | bytes 6148
  (80 other events, 62.7 us)
Sparse Core Ops, SparseCore 0:
  109.7 61.1 reduce-scatter.10
  174.7 59.1 reduce-scatter.8
  237.6 59.1 reduce-scatter.6
  300.4 59.1 reduce-scatter.4
where the time goes:
time: 370 us; the launch traced here: 368 us
  waiting for transfers between devices  180 us (49%)
  Pallas kernels  99.3 us (27%)
  local copies, waits for them, and re-layouts  68.1 us (18%)
  between operations  14.3 us (4%)
  other arithmetic  6.38 us (2%)
    reduce_scatter x4, waiting for transfers between devices, body(): lax.psum_scatter(term.reshape(27, chans, chans), ('ha', 'wa'), scatter_di...  180 us
    pallas_call x9, Pallas kernels, exchange(): pl.pallas_call(run, out_shape=(jax.ShapeDtypeStruct((n,) + stat.shape, jn...  88.3 us
    unnamed x200, local copies, waits for them, and re-layouts  63.9 us
    pallas_call x9, Pallas kernels, call(): pl.pallas_call(body, out_shape=tuple((jax.ShapeDtypeStruct(shape, dtype)...  11 us
  transfers between devices with their start and end apart: 4, of which 3 were waited for; matrix products, arithmetic and copies ran while one was open for 1% of the time, Pallas kernels for 12%

commit v1 on v0

--- a/solution.py
+++ b/solution.py
@@ -271,6 +271,93 @@
     )(*args)
 
 
+def scatter_kernel(*refs, layers, rows_n, scale):
+    terms, refs = refs[:layers], refs[layers:]
+    result, got0, sum0, got1, sum1, got2, send0, recv0, send1, recv1, send2, recv2 = refs
+    g, a, w = lax.axis_index("grp"), lax.axis_index("ha"), lax.axis_index("wa")
+    low, high = lax.rem(w, 2), lax.div(w, 2)
+    near = (g, a, w + 1 - 2 * low)
+    far = (g, a, w + 2 - 4 * high)
+    rows_to = [lax.rem(a + k, rows_n) for k in range(rows_n)]
+    barrier = pltpu.get_barrier_semaphore()
+    for device in [near, far] + [(g, rows_to[k], w) for k in range(1, rows_n)]:
+        pl.semaphore_signal(barrier, inc=1, device_id=device, device_id_type=MESH)
+    pl.semaphore_wait(barrier, rows_n + 1)
+
+    def send(src, dst, send_sem, recv_sem, device):
+        copy = pltpu.make_async_remote_copy(src, dst, send_sem, recv_sem, device_id=device, device_id_type=MESH)
+        copy.start()
+        return copy
+
+    first = [
+        send(terms[j].at[1 - low], got0.at[j], send0.at[j], recv0.at[j], near) for j in range(layers)
+    ]
+    second, third = [], []
+    for j in range(layers):
+        first[j].wait()
+        for b in range(2):
+            total = terms[j][low, b].astype(jnp.float32) + got0[j, b].astype(jnp.float32)
+            sum0[j, b] = total.astype(jnp.bfloat16)
+        second.append(send(sum0.at[j, 1 - high], got1.at[j], send1.at[j], recv1.at[j], far))
+    for j in range(layers):
+        second[j].wait()
+        total = sum0[j, high].astype(jnp.float32) + got1[j].astype(jnp.float32)
+        sum1[j] = total.astype(jnp.bfloat16)
+        third.append(
+            [
+                send(sum1.at[j, rows_to[k]], got2.at[j, k], send2.at[j, k], recv2.at[j, k], (g, rows_to[k], w))
+                for k in range(1, rows_n)
+            ]
+        )
+    for j in range(layers):
+        total = sum1[j, a].astype(jnp.float32)
+        for k in range(1, rows_n):
+            third[j][k - 1].wait()
+            total = total + got2[j, k].astype(jnp.float32)
+        result[j] = total * scale
+
+
+def scatter_terms(terms, chans, rows_n, cols_n, scale):
+    layers = len(terms)
+    share = chans // (rows_n * cols_n)
+    size = 16 * pl.cdiv(27 * share, 16)
+    shape = (2, 2, rows_n, size, chans)
+    vmem = pl.BlockSpec(memory_space=pltpu.VMEM)
+    dma = pltpu.SemaphoreType.DMA
+
+    def run(*refs):
+        scatter_kernel(*refs, layers=layers, rows_n=rows_n, scale=scale)
+
+    out = pl.pallas_call(
+        run,
+        out_shape=jax.ShapeDtypeStruct((layers, size, chans), jnp.float32),
+        in_specs=[vmem] * layers,
+        out_specs=vmem,
+        scratch_shapes=[
+            pltpu.VMEM((layers,) + shape[1:], jnp.bfloat16),
+            pltpu.VMEM((layers,) + shape[1:], jnp.bfloat16),
+            pltpu.VMEM((layers,) + shape[2:], jnp.bfloat16),
+            pltpu.VMEM((layers,) + shape[2:], jnp.bfloat16),
+            pltpu.VMEM((layers,) + shape[2:], jnp.bfloat16),
+            dma((layers,)),
+            dma((layers,)),
+            dma((layers,)),
+            dma((layers,)),
+            dma((layers, rows_n)),
+            dma((layers, rows_n)),
+        ],
+        compiler_params=pltpu.CompilerParams(collective_id=1, has_side_effects=True, vmem_limit_bytes=40 * 2**20),
+    )(*terms)
+    return out[:, : 27 * share].reshape(layers, 27, share * chans)
+
+
+def spread_shares(term, chans, rows_n, cols_n):
+    share = chans // (rows_n * cols_n)
+    parts = term.reshape(27, rows_n, 2, 2, share, chans).transpose(3, 2, 1, 0, 4, 5)
+    parts = parts.reshape(2, 2, rows_n, 27 * share, chans).astype(jnp.bfloat16)
+    return jnp.pad(parts, ((0, 0), (0, 0), (0, 0), (0, -27 * share % 16), (0, 0)))
+
+
 def body(inputs, upstream, kernels, norm_gain, norm_shift):
     frames, rows, width, chans = inputs.shape
     rows_n, cols_n = lax.axis_size("ha"), lax.axis_size("wa")
@@ -349,8 +436,7 @@
         )
         if layer % 2 == 1:
             grad_stream = keep
-        share = lax.psum_scatter(term.reshape(27, chans, chans), ("ha", "wa"), scatter_dimension=1, tiled=True)
-        terms[layer] = share.reshape(27, -1)
+        terms[layer] = spread_shares(term, chans, rows_n, cols_n)
     all_stat, _ = exchange(stat, edges, plan, rows_n, cols_n)
     total = jnp.sum(all_stat, axis=0)
     shift_sums[0] = jnp.sum(total[:frames], axis=0)
@@ -361,7 +447,8 @@
     into = saved[0][1][:, None, None] * (values * norm_gain[0] - s1 - saved[0][0][cut] * s2)
     input_grad = (grad_stream[cut] + into).astype(jnp.bfloat16)
     norm_grads = jnp.stack([jnp.stack(gain_sums), jnp.stack(shift_sums)]) * scale
-    return (input_grad, jnp.stack(terms) * scale, norm_grads)
+    kernel_grads = scatter_terms(terms, chans, rows_n, cols_n, scale)
+    return (input_grad, kernel_grads, norm_grads)
 
 
 def solution(mesh):

time: 370 us -> 220 us (0.59)
  waiting for transfers between devices: 180 us -> 0 us
  Pallas kernels: 99.3 us -> 131 us
  between operations: 14.3 us -> 1.24 us
  local copies, waits for them, and re-layouts: 68.1 us -> 79.6 us
    reduce_scatter x4 -> x0, waiting for transfers between devices: 180 us -> none  [body(): lax.psum_scatter(term.reshape(27, chans, chans), ('ha', 'wa'), scatter_di...]
    pallas_call x0 -> x1, Pallas kernels: none -> 33 us  [scatter_terms(): pl.pallas_call(run, out_shape=jax.ShapeDtypeStruct((layers, size, chans),...]
    unnamed x200 -> x207, local copies, waits for them, and re-layouts: 63.9 us -> 73.4 us
  transfers between devices with their start and end apart: 4 -> 0, of which waited for: 3 -> 0; matrix products, arithmetic and copies ran while one was open for 1% -> 0% of each run, Pallas kernels for 12% -> 0%
where the time goes in v1:
time: 220 us; the launch traced here: 218 us
  Pallas kernels  131 us (60%)
  local copies, waits for them, and re-layouts  79.6 us (36%)
  other arithmetic  6.08 us (3%)
    pallas_call x9, Pallas kernels, exchange(): pl.pallas_call(run, out_shape=(jax.ShapeDtypeStruct((n,) + stat.shape, jn...  88.1 us
    unnamed x207, local copies, waits for them, and re-layouts  73.4 us
    pallas_call x1, Pallas kernels, scatter_terms(): pl.pallas_call(run, out_shape=jax.ShapeDtypeStruct((layers, size, chans),...  33 us
    pallas_call x9, Pallas kernels, call(): pl.pallas_call(body, out_shape=tuple((jax.ShapeDtypeStruct(shape, dtype)...  10.1 us

profile of v1, /device:TPU:0, one launch (start us, length us, event | category | flops | bytes accessed | tf_op | source)
XLA Modules:
  0.0 218.1 jit_solution(7241643395324932681)
XLA Ops:
  0.7 1.5 slice_bitcast_fusion.4
  8.5 11.6 %shard_map.77 = (f32[16,8,128]{2,1,0:T(8,128)}, f32[192,128]{1,0:T(8,128)}) custom-call(f32[8,128]{1,0:T(8,128)} %broadcast_in_dim.4.args_0_, f32[192,128]{1,0:T(8,128)} %copy-done.64), custom_call_target="tpu_custom_call" | custom-call | tf_op jit(solution)/shard_map/pallas_call | solution.py:89
  20.1 9.3 %shard_map.78 = (f32[16,8,128]{2,1,0:T(8,128)}, f32[192,128]{1,0:T(8,128)}) custom-call(f32[8,128]{1,0:T(8,128)} %copy-done.87, f32[192,128]{1,0:T(8,128)} %copy-done.59), custom_call_target="tpu_custom_call" | custom-call | tf_op jit(solution)/shard_map/pallas_call | solution.py:89
  29.5 2.3 %slice_bitcast_fusion = (bf16[3456,128]{1,0:T(8,128)(2,1)S(1)}, bf16[3456,128]{1,0:T(8,128)(2,1)S(1)}, bf16[3456,128]{1,0:T(8,128)(2,1)S(1)}, bf16[3456,128]{1,0:T(8,128)(2,1)S(1)}) fusion(bf16[4,3456,128]{2,1,0:T(8,128)(2,1)} %param.7), kind=kLoop, calls=%fused_computation.4 | loop fusion | bytes 7077888 | tf_op jit(solution)/shard_map/squeeze | solution.py:393
  37.2 9.6 %shard_map.80 = (f32[16,8,128]{2,1,0:T(8,128)}, f32[192,128]{1,0:T(8,128)}) custom-call(f32[8,128]{1,0:T(8,128)} %copy-done.91, f32[192,128]{1,0:T(8,128)} %copy-done.63), custom_call_target="tpu_custom_call" | custom-call | tf_op jit(solution)/shard_map/pallas_call | solution.py:89
  52.8 1.2 copy-done.7
  57.3 9.6 %shard_map.82 = (f32[16,8,128]{2,1,0:T(8,128)}, f32[192,128]{1,0:T(8,128)}) custom-call(f32[8,128]{1,0:T(8,128)} %copy-done.89, f32[192,128]{1,0:T(8,128)} %copy-done.61), custom_call_target="tpu_custom_call" | custom-call | tf_op jit(solution)/shard_map/pallas_call | solution.py:89
  76.5 9.6 %shard_map.84 = (f32[16,8,128]{2,1,0:T(8,128)}, f32[192,128]{1,0:T(8,128)}) custom-call(f32[8,128]{1,0:T(8,128)} %copy-done.90, f32[192,128]{1,0:T(8,128)} %copy-done.62), custom_call_target="tpu_custom_call" | custom-call | tf_op jit(solution)/shard_map/pallas_call | solution.py:89
  95.6 1.4 shard_map.86
  100.9 9.6 %shard_map.87 = (f32[16,8,128]{2,1,0:T(8,128)}, f32[192,128]{1,0:T(8,128)}) custom-call(f32[8,128]{1,0:T(8,128)} %copy-done.88, f32[192,128]{1,0:T(8,128)} %copy-done.60), custom_call_target="tpu_custom_call" | custom-call | tf_op jit(solution)/shard_map/pallas_call | solution.py:89
  111.4 1.5 copy-done.18
  118.8 1.8 shard_map.88
  125.0 9.6 %shard_map.89 = (f32[16,8,128]{2,1,0:T(8,128)}, f32[192,128]{1,0:T(8,128)}) custom-call(f32[8,128]{1,0:T(8,128)} %copy-done.86, f32[192,128]{1,0:T(8,128)} %copy-done.58), custom_call_target="tpu_custom_call" | custom-call | tf_op jit(solution)/shard_map/pallas_call | solution.py:89
  134.7 1.5 copy-done.8
  141.0 1.5 shard_map.90
  142.6 1.2 copy-done.15
  147.4 9.6 %shard_map.91 = (f32[16,8,128]{2,1,0:T(8,128)}, f32[192,128]{1,0:T(8,128)}) custom-call(f32[8,128]{1,0:T(8,128)} %copy-done.85, f32[192,128]{1,0:T(8,128)} %copy-done.57), custom_call_target="tpu_custom_call" | custom-call | tf_op jit(solution)/shard_map/pallas_call | solution.py:89
  157.0 1.5 copy-done.12
  162.8 1.8 shard_map.92
  165.8 9.6 %shard_map.93 = (f32[16,8,128]{2,1,0:T(8,128)}, f32[192,128]{1,0:T(8,128)}) custom-call(f32[8,128]{1,0:T(8,128)} %copy-done.84, f32[192,128]{1,0:T(8,128)} %copy-done.56), custom_call_target="tpu_custom_call" | custom-call | tf_op jit(solution)/shard_map/pallas_call | solution.py:89
  177.1 1.7 add_convert_fusion
  179.2 1.2 copy-done.16
  180.7 1.2 copy-done.14
  183.9 33.0 %shard_map.94 = f32[4,224,128]{2,1,0:T(8,128)S(1)} custom-call(bf16[2,2,4,224,128]{4,3,2,1,0:T(8,128)(2,1)S(1)} %pad.13.refs_0_, bf16[2,2,4,224,128]{4,3,2,1,0:T(8,128)(2,1)S(1)} %pad.14.refs_1_, bf16[2,2,4,224,128]{4,3,2,1,0:T(8,128)(2,1)S(1)} %pad.15.refs_2_, bf16[2,2,4,224,128]{4,3,2,1,0:T(8,128)(2,1)S(1)} %pad.16.refs_3_), custom_call_target="tpu_custom_call" | custom-call | tf_op jit(solution)/shard_map/pallas_call | solution.py:331
  (237 shorter events, 74.3 us)
Async XLA Ops:
  29.4 2.4 %copy-start = (f32[6,32,128]{2,1,0:T(8,128)S(1)}, f32[6,32,128]{2,1,0:T(8,128)}, u32[]{:S(2)}) copy-start(f32[6,32,128]{2,1,0:T(8,128)} %broadcast_in_dim.5.r_3_) | copy-start | bytes 294916
  29.5 2.4 %copy-start.29 = (f32[4,4,16,128]{3,2,1,0:T(8,128)S(1)}, f32[4,4,16,128]{3,2,1,0:T(8,128)}, u32[]{:S(2)}) copy-start(f32[4,4,16,128]{3,2,1,0:T(8,128)} %copy-done.28) | copy-start | bytes 393220
  29.5 2.4 %copy-start.52 = (f32[192,128]{1,0:T(8,128)S(1)}, f32[192,128]{1,0:T(8,128)}, u32[]{:S(2)}) copy-start(f32[192,128]{1,0:T(8,128)} %get-tuple-element.71.r_1_) | copy-start | bytes 294916
  29.5 2.4 %copy-start.69 = (f32[16,8,128]{2,1,0:T(8,128)S(1)}, f32[16,8,128]{2,1,0:T(8,128)}, u32[]{:S(2)}) copy-start(f32[16,8,128]{2,1,0:T(8,128)} %get-tuple-element.72.r_2_) | copy-start | bytes 196612
  29.5 2.4 %copy-start.76 = (f32[1,128]{1,0:T(1,128)S(1)}, f32[1,128]{1,0:T(1,128)}, u32[]{:S(2)}) copy-start(f32[1,128]{1,0:T(1,128)} %get-tuple-element.161.r_6_) | copy-start | bytes 1540
  52.8 1.3 copy-start.7
  72.0 1.2 copy-start.17
  91.4 5.7 %copy-start.24 = (f32[4,6,32,128]{3,2,1,0:T(8,128)}, f32[4,6,32,128]{3,2,1,0:T(8,128)S(1)}, u32[]{:S(2)}) copy-start(f32[4,6,32,128]{3,2,1,0:T(8,128)S(1)} %get-tuple-element.88.r_7_.r_9_) | copy-start | bytes 1179652
  111.4 1.5 copy-start.18
  118.8 15.9 %copy-start.6 = (f32[6,32,128]{2,1,0:T(8,128)S(1)}, f32[6,32,128]{2,1,0:T(8,128)}, u32[]{:S(2)}) copy-start(f32[6,32,128]{2,1,0:T(8,128)} %broadcast_in_dim.5.r_3_) | copy-start | bytes 294916
  118.8 15.9 %copy-start.20 = (f32[4,6,32,128]{3,2,1,0:T(8,128)S(1)}, f32[4,6,32,128]{3,2,1,0:T(8,128)}, u32[]{:S(2)}) copy-start(f32[4,6,32,128]{3,2,1,0:T(8,128)} %copy-done.19) | copy-start | bytes 1179652
  118.8 15.9 %copy-start.23 = (f32[4,6,32,128]{3,2,1,0:T(8,128)S(1)}, f32[4,6,32,128]{3,2,1,0:T(8,128)}, u32[]{:S(2)}) copy-start(f32[4,6,32,128]{3,2,1,0:T(8,128)} %copy-done.21) | copy-start | bytes 1179652
  134.7 1.5 copy-start.8
  141.0 16.0 %copy-start.77 = (f32[1,128]{1,0:T(1,128)S(1)}, f32[1,128]{1,0:T(1,128)}, u32[]{:S(2)}) copy-start(f32[1,128]{1,0:T(1,128)} %get-tuple-element.161.r_6_) | copy-start | bytes 1540
  142.6 1.3 copy-start.15
  157.0 1.5 copy-start.12
  162.8 3.0 %copy-start.34 = (f32[16,8,128]{2,1,0:T(8,128)S(1)}, f32[16,8,128]{2,1,0:T(8,128)}, u32[]{:S(2)}) copy-start(f32[16,8,128]{2,1,0:T(8,128)} %get-tuple-element.113.r_2_) | copy-start | bytes 196612
  162.8 13.5 %copy-start.100 = (f32[128]{0:T(128)S(1)}, f32[128]{0:T(128)}, u32[]{:S(2)}) copy-start(f32[128]{0:T(128)} %get-tuple-element.150) | copy-start | bytes 1540
  162.8 13.7 %copy-start.102 = (f32[128]{0:T(128)S(1)}, f32[128]{0:T(128)}, u32[]{:S(2)}) copy-start(f32[128]{0:T(128)} %get-tuple-element.144) | copy-start | bytes 1540
  162.8 13.7 %copy-start.101 = (f32[128]{0:T(128)S(1)}, f32[128]{0:T(128)}, u32[]{:S(2)}) copy-start(f32[128]{0:T(128)} %get-tuple-element.145) | copy-start | bytes 1540
  162.8 14.3 %copy-start.93 = (f32[4,128]{1,0:T(4,128)S(1)}, f32[4,128]{1,0:T(4,128)}, u32[]{:S(2)}) copy-start(f32[4,128]{1,0:T(4,128)} %copy-done.92) | copy-start | bytes 6148
  178.9 1.5 copy-start.16
  180.5 1.5 copy-start.14
  182.0 1.5 copy-start.10
  (79 other events, 60.6 us)

commit v2 on v1

--- a/solution.py
+++ b/solution.py
@@ -78,8 +78,8 @@
     return plan, offset
 
 
-def exchange(stat, packed, plan, rows_n, cols_n):
-    pieces = [(dh, dw, start, start, size) for (dh, dw), (start, size) in plan.items()]
+def exchange(stat, packed, plans, rows_n, cols_n, collective_id):
+    pieces = [(dh, dw, start, start, size) for plan in plans for (dh, dw), (start, size) in plan.items()]
     n = rows_n * cols_n
     vmem = pl.BlockSpec(memory_space=pltpu.VMEM)
 
@@ -97,10 +97,10 @@
         scratch_shapes=[
             pltpu.SemaphoreType.DMA((n,)),
             pltpu.SemaphoreType.DMA((n,)),
-            pltpu.SemaphoreType.DMA((8,)),
-            pltpu.SemaphoreType.DMA((8,)),
+            pltpu.SemaphoreType.DMA((len(pieces),)),
+            pltpu.SemaphoreType.DMA((len(pieces),)),
         ],
-        compiler_params=pltpu.CompilerParams(collective_id=0, has_side_effects=True),
+        compiler_params=pltpu.CompilerParams(collective_id=collective_id, has_side_effects=True),
     )(stat, packed)
 
 
@@ -203,15 +203,15 @@
     stat[frames:] = jnp.sum(centred * centred, axis=(1, 2))
 
 
-def start_kernel(inputs, upstream, values, up, stat, edges, up_edges, *, plan):
+def start_kernel(inputs, upstream, values, up, stat, edges, *, plan, up_plan):
     values[...] = inputs[...].astype(jnp.float32)
     up[...] = upstream[...].astype(jnp.float32)
     fill_stat(stat, values[...])
     pack(edges, values, plan)
-    pack(up_edges, up, plan)
-
-
-def backward_kernel(*refs, plan, count, normed_in, add):
+    pack(edges, up, up_plan)
+
+
+def backward_kernel(*refs, plan, from_plan, count, normed_in, add):
     refs = list(refs)
     values, border, all_stat, mask, kernel, gain, shift, normed, patches = refs[:9]
     refs = refs[9:]
@@ -221,7 +221,7 @@
     base = refs.pop(0) if add else None
     keep, term, dn_out, stat, edges, wide, shifted, out_patches = refs
     frames, rows, width, chans = values.shape
-    unpack(wide, values, border, plan)
+    unpack(wide, values, border, from_plan)
     if normed_in:
         total = jnp.sum(all_stat[...], axis=0)
         s1 = total_mean(total[:frames] * last_gain[...], count)
@@ -267,7 +267,7 @@
         in_specs=[vmem] * len(args),
         out_specs=(vmem,) * len(outs),
         scratch_shapes=[pltpu.VMEM(shape, dtype) for shape, dtype in scratch],
-        compiler_params=pltpu.CompilerParams(vmem_limit_bytes=40 * 2**20),
+        compiler_params=pltpu.CompilerParams(vmem_limit_bytes=58 * 2**20),
     )(*args)
 
 
@@ -346,7 +346,7 @@
             dma((layers, rows_n)),
             dma((layers, rows_n)),
         ],
-        compiler_params=pltpu.CompilerParams(collective_id=1, has_side_effects=True, vmem_limit_bytes=40 * 2**20),
+        compiler_params=pltpu.CompilerParams(collective_id=1, has_side_effects=True, vmem_limit_bytes=58 * 2**20),
     )(*terms)
     return out[:, : 27 * share].reshape(layers, 27, share * chans)
 
@@ -381,13 +381,21 @@
     gains = [norm_gain[j : j + 1] for j in range(layers)]
     shifts = [norm_shift[j : j + 1] for j in range(layers)]
 
-    values, up, stat, edges, up_edges = call(
-        lambda *r: start_kernel(*r, plan=plan), [inputs, upstream], [own, own, stat_t, edge_t, edge_t], []
+    up_plan = {key: (start + edge_rows, size) for key, (start, size) in plan.items()}
+    values, up, stat, edges = call(
+        lambda *r: start_kernel(*r, plan=plan, up_plan=up_plan),
+        [inputs, upstream],
+        [own, own, stat_t, ((2 * edge_rows, chans), f32)],
+        [],
     )
     stream = values
     saved = []
     for layer in range(layers):
-        all_stat, border = exchange(stat, edges, plan, rows_n, cols_n)
+        if layer == 0:
+            all_stat, border = exchange(stat, edges, [plan, up_plan], rows_n, cols_n, 2)
+            up_stat, up_border = all_stat, border
+        else:
+            all_stat, border = exchange(stat, edges, [plan], rows_n, cols_n, 0)
         add = layer % 2 == 1 and layer < layers - 1
         conv = layer < layers - 1
         args = [values, border, all_stat, mask, kernels[layer], gains[layer], shifts[layer]]
@@ -406,10 +414,13 @@
                 stream = values
 
     terms, gain_sums, shift_sums = [None] * layers, [None] * layers, [None] * layers
-    values, edges, stat = up, up_edges, jnp.zeros(stat_t[0], f32)
+    values = up
     grad_stream = None
     for layer in range(layers - 1, -1, -1):
-        all_stat, border = exchange(stat, edges, plan, rows_n, cols_n)
+        if layer == layers - 1:
+            all_stat, border = up_stat, up_border
+        else:
+            all_stat, border = exchange(stat, edges, [plan], rows_n, cols_n, 0)
         args = [values, border, all_stat, mask, kernels[layer], gains[layer], shifts[layer], saved[layer][0], saved[layer][2]]
         normed_in = layer < layers - 1
         add = normed_in and layer % 2 == 1
@@ -421,8 +432,10 @@
         if add:
             args.append(grad_stream)
 
-        def run_back(*r, normed_in=normed_in, add=add):
-            backward_kernel(*r, plan=plan, count=count, normed_in=normed_in, add=add)
+        from_plan = plan if normed_in else up_plan
+
+        def run_back(*r, normed_in=normed_in, add=add, from_plan=from_plan):
+            backward_kernel(*r, plan=plan, from_plan=from_plan, count=count, normed_in=normed_in, add=add)
 
         keep, term, values, stat, edges = call(
             run_back,
@@ -437,7 +450,7 @@
         if layer % 2 == 1:
             grad_stream = keep
         terms[layer] = spread_shares(term, chans, rows_n, cols_n)
-    all_stat, _ = exchange(stat, edges, plan, rows_n, cols_n)
+    all_stat, _ = exchange(stat, edges, [plan], rows_n, cols_n, 0)
     total = jnp.sum(all_stat, axis=0)
     shift_sums[0] = jnp.sum(total[:frames], axis=0)
     gain_sums[0] = jnp.sum(total[frames:], axis=0)

time: 220 us -> 172 us (0.78)
  local copies, waits for them, and re-layouts: 79.6 us -> 14.7 us
  Pallas kernels: 131 us -> 150 us
    unnamed x207 -> x15, local copies, waits for them, and re-layouts: 73.4 us -> 3 us
    pallas_call x9, Pallas kernels: 10.1 us -> 34.9 us  [call(): pl.pallas_call(body, out_shape=tuple((jax.ShapeDtypeStruct(shape, dtype)...]
    pallas_call x9 -> x8, Pallas kernels: 88.1 us -> 79.6 us  [exchange(): pl.pallas_call(run, out_shape=(jax.ShapeDtypeStruct((n,) + stat.shape, jn...]
    pad x4, local copies, waits for them, and re-layouts: 0.26 us -> 4.02 us  [spread_shares(): jnp.pad(parts, ((0, 0), (0, 0), (0, 0), (0, -27 * share % 16), (0, 0)))]
    pallas_call x1, Pallas kernels: 33 us -> 35.7 us  [scatter_terms(): pl.pallas_call(run, out_shape=jax.ShapeDtypeStruct((layers, size, chans),...]
where the time goes in v2:
time: 172 us; the launch traced here: 171 us
  Pallas kernels  150 us (87%)
  local copies, waits for them, and re-layouts  14.7 us (9%)
  other arithmetic  5.44 us (3%)
    pallas_call x8, Pallas kernels, exchange(): pl.pallas_call(run, out_shape=(jax.ShapeDtypeStruct((n,) + stat.shape, jn...  79.6 us
    pallas_call x1, Pallas kernels, scatter_terms(): pl.pallas_call(run, out_shape=jax.ShapeDtypeStruct((layers, size, chans),...  35.7 us
    pallas_call x9, Pallas kernels, call(): pl.pallas_call(body, out_shape=tuple((jax.ShapeDtypeStruct(shape, dtype)...  34.9 us
    pad x4, local copies, waits for them, and re-layouts, spread_shares(): jnp.pad(parts, ((0, 0), (0, 0), (0, 0), (0, -27 * share % 16), (0, 0)))  4.02 us
    squeeze x1, local copies, waits for them, and re-layouts, body(): kernels[layer]  3.79 us

profile of v2, /device:TPU:0, one launch (start us, length us, event | category | flops | bytes accessed | tf_op | source)
XLA Modules:
  0.0 171.2 jit_solution(283677493359407210)
XLA Ops:
  0.7 1.5 slice_bitcast_fusion.4
  2.9 1.6 shard_map.76
  4.6 12.7 %shard_map.77 = (f32[16,8,128]{2,1,0:T(8,128)}, f32[384,128]{1,0:T(8,128)}) custom-call(f32[8,128]{1,0:T(8,128)} %get-tuple-element.62.args_0_, f32[384,128]{1,0:T(8,128)} %get-tuple-element.63.args_1_), custom_call_target="tpu_custom_call" | custom-call | tf_op jit(solution)/shard_map/pallas_call | solution.py:89
  17.3 3.8 %slice_bitcast_fusion = (bf16[3456,128]{1,0:T(8,128)(2,1)}, bf16[3456,128]{1,0:T(8,128)(2,1)}, bf16[3456,128]{1,0:T(8,128)(2,1)}, bf16[3456,128]{1,0:T(8,128)(2,1)}) fusion(bf16[4,3456,128]{2,1,0:T(8,128)(2,1)} %param.7), kind=kLoop, calls=%fused_computation.4 | loop fusion | bytes 7077888 | tf_op jit(solution)/shard_map/squeeze | solution.py:401
  21.1 3.5 %shard_map.78 = (f32[4,6,32,128]{3,2,1,0:T(8,128)}, f32[4,128]{1,0:T(4,128)}, bf16[256,3456]{1,0:T(8,128)(2,1)}, f32[4,4,16,128]{3,2,1,0:T(8,128)}, f32[8,128]{1,0:T(8,128)}, /*index=5*/f32[192,128]{1,0:T(8,128)}) custom-call(f32[4,4,16,128]{3,2,1,0:T(8,128)} %get-tuple-element.66.r_0_.r_7_, f32[384,128]{1,0:T(8,128)} %get-tuple-element.64.r_1_, ...), custom_call_target="tpu_custom_call" | custom-call | tf_op jit(solution)/shard_map/pallas_call | solution.py:264
  24.6 9.3 %shard_map.79 = (f32[16,8,128]{2,1,0:T(8,128)}, f32[192,128]{1,0:T(8,128)}) custom-call(f32[8,128]{1,0:T(8,128)} %get-tuple-element.68.args_0_, f32[192,128]{1,0:T(8,128)} %get-tuple-element.69.args_1_), custom_call_target="tpu_custom_call" | custom-call | tf_op jit(solution)/shard_map/pallas_call | solution.py:89
  33.9 3.5 %shard_map.80 = (f32[4,6,32,128]{3,2,1,0:T(8,128)}, f32[4,128]{1,0:T(4,128)}, bf16[256,3456]{1,0:T(8,128)(2,1)}, f32[4,4,16,128]{3,2,1,0:T(8,128)}, f32[8,128]{1,0:T(8,128)}, /*index=5*/f32[192,128]{1,0:T(8,128)}) custom-call(f32[4,4,16,128]{3,2,1,0:T(8,128)} %get-tuple-element.67.r_0_, f32[192,128]{1,0:T(8,128)} %get-tuple-element.70.r_1_, ...), custom_call_target="tpu_custom_call" | custom-call | tf_op jit(solution)/shard_map/pallas_call | solution.py:264
  37.4 9.8 %shard_map.81 = (f32[16,8,128]{2,1,0:T(8,128)}, f32[192,128]{1,0:T(8,128)}) custom-call(f32[8,128]{1,0:T(8,128)} %get-tuple-element.73.args_0_, f32[192,128]{1,0:T(8,128)} %get-tuple-element.74.args_1_), custom_call_target="tpu_custom_call" | custom-call | tf_op jit(solution)/shard_map/pallas_call | solution.py:89
  47.1 3.5 %shard_map.82 = (f32[4,6,32,128]{3,2,1,0:T(8,128)}, f32[4,128]{1,0:T(4,128)}, bf16[256,3456]{1,0:T(8,128)(2,1)}, f32[4,4,16,128]{3,2,1,0:T(8,128)}, f32[8,128]{1,0:T(8,128)}, /*index=5*/f32[192,128]{1,0:T(8,128)}) custom-call(f32[4,4,16,128]{3,2,1,0:T(8,128)} %get-tuple-element.72.r_0_, f32[192,128]{1,0:T(8,128)} %get-tuple-element.75.r_1_, ...), custom_call_target="tpu_custom_call" | custom-call | tf_op jit(solution)/shard_map/pallas_call | solution.py:264
  50.7 9.3 %shard_map.83 = (f32[16,8,128]{2,1,0:T(8,128)}, f32[192,128]{1,0:T(8,128)}) custom-call(f32[8,128]{1,0:T(8,128)} %get-tuple-element.78.args_0_, f32[192,128]{1,0:T(8,128)} %get-tuple-element.79.args_1_), custom_call_target="tpu_custom_call" | custom-call | tf_op jit(solution)/shard_map/pallas_call | solution.py:89
  60.0 3.2 %shard_map.84 = (f32[4,6,32,128]{3,2,1,0:T(8,128)}, f32[4,128]{1,0:T(4,128)}, bf16[256,3456]{1,0:T(8,128)(2,1)}) custom-call(f32[4,4,16,128]{3,2,1,0:T(8,128)} %get-tuple-element.77.r_0_, f32[192,128]{1,0:T(8,128)} %get-tuple-element.80.r_1_, f32[16,8,128]{2,1,0:T(8,128)} %get-tuple-element.81.r_2_, f32[6,32,128]{2,1,0:T(8,128)} %broadcast_in_dim.2.r_3_, ...), custom_call_target="tpu_custom_call" | custom-call | tf_op jit(solution)/shard_map/pallas_call | solution.py:264
  63.2 4.7 %shard_map.85 = (f32[4,6,32,128]{3,2,1,0:T(8,128)}, f32[3456,128]{1,0:T(8,128)}, f32[4,4,16,128]{3,2,1,0:T(8,128)}, f32[8,128]{1,0:T(8,128)}, f32[192,128]{1,0:T(8,128)}) custom-call(f32[4,4,16,128]{3,2,1,0:T(8,128)} %get-tuple-element.61.r_0_, f32[384,128]{1,0:T(8,128)} %get-tuple-element.64.r_1_, f32[16,8,128]{2,1,0:T(8,128)} %get-tuple-element.65.r_2_, ...), custom_call_target="tpu_custom_call" | custom-call | tf_op jit(solution)/shard_map/pallas_call | solution.py:264
  67.9 9.6 %shard_map.86 = (f32[16,8,128]{2,1,0:T(8,128)}, f32[192,128]{1,0:T(8,128)}) custom-call(f32[8,128]{1,0:T(8,128)} %get-tuple-element.85.args_0_, f32[192,128]{1,0:T(8,128)} %get-tuple-element.86.args_1_), custom_call_target="tpu_custom_call" | custom-call | tf_op jit(solution)/shard_map/pallas_call | solution.py:89
  77.5 4.9 %shard_map.87 = (f32[4,6,32,128]{3,2,1,0:T(8,128)}, f32[3456,128]{1,0:T(8,128)}, f32[4,4,16,128]{3,2,1,0:T(8,128)}, f32[8,128]{1,0:T(8,128)}, f32[192,128]{1,0:T(8,128)}) custom-call(f32[4,4,16,128]{3,2,1,0:T(8,128)} %get-tuple-element.84.r_0_, f32[192,128]{1,0:T(8,128)} %get-tuple-element.87.r_1_, f32[16,8,128]{2,1,0:T(8,128)} %get-tuple-element.88.r_2_, ...), custom_call_target="tpu_custom_call" | custom-call | tf_op jit(solution)/shard_map/pallas_call | solution.py:264
  82.4 9.6 %shard_map.88 = (f32[16,8,128]{2,1,0:T(8,128)}, f32[192,128]{1,0:T(8,128)}) custom-call(f32[8,128]{1,0:T(8,128)} %get-tuple-element.93.args_0_, f32[192,128]{1,0:T(8,128)} %get-tuple-element.94.args_1_), custom_call_target="tpu_custom_call" | custom-call | tf_op jit(solution)/shard_map/pallas_call | solution.py:89
  92.1 5.0 %shard_map.89 = (f32[4,6,32,128]{3,2,1,0:T(8,128)}, f32[3456,128]{1,0:T(8,128)}, f32[4,4,16,128]{3,2,1,0:T(8,128)}, f32[8,128]{1,0:T(8,128)}, f32[192,128]{1,0:T(8,128)}) custom-call(f32[4,4,16,128]{3,2,1,0:T(8,128)} %get-tuple-element.92.r_0_, f32[192,128]{1,0:T(8,128)} %get-tuple-element.95.r_1_, f32[16,8,128]{2,1,0:T(8,128)} %get-tuple-element.96.r_2_, ...), custom_call_target="tpu_custom_call" | custom-call | tf_op jit(solution)/shard_map/pallas_call | solution.py:264
  97.1 9.6 %shard_map.90 = (f32[16,8,128]{2,1,0:T(8,128)}, f32[192,128]{1,0:T(8,128)}) custom-call(f32[8,128]{1,0:T(8,128)} %get-tuple-element.104.args_0_, f32[192,128]{1,0:T(8,128)} %get-tuple-element.105.args_1_), custom_call_target="tpu_custom_call" | custom-call | tf_op jit(solution)/shard_map/pallas_call | solution.py:89
  106.7 5.1 %shard_map.91 = (f32[4,6,32,128]{3,2,1,0:T(8,128)}, f32[3456,128]{1,0:T(8,128)}, f32[4,4,16,128]{3,2,1,0:T(8,128)}, f32[8,128]{1,0:T(8,128)}, f32[192,128]{1,0:T(8,128)}) custom-call(f32[4,4,16,128]{3,2,1,0:T(8,128)} %get-tuple-element.103.r_0_, f32[192,128]{1,0:T(8,128)} %get-tuple-element.106.r_1_, f32[16,8,128]{2,1,0:T(8,128)} %get-tuple-element.107.r_2_, ...), custom_call_target="tpu_custom_call" | custom-call | tf_op jit(solution)/shard_map/pallas_call | solution.py:264
  111.8 9.6 %shard_map.92 = (f32[16,8,128]{2,1,0:T(8,128)}, f32[192,128]{1,0:T(8,128)}) custom-call(f32[8,128]{1,0:T(8,128)} %get-tuple-element.112.args_0_, f32[192,128]{1,0:T(8,128)} %get-tuple-element.113.args_1_), custom_call_target="tpu_custom_call" | custom-call | tf_op jit(solution)/shard_map/pallas_call | solution.py:89
  123.1 1.8 %add_convert_fusion = bf16[4,4,16,128]{3,2,1,0:T(8,128)(2,1)} fusion(f32[4,6,32,128]{3,2,1,0:T(8,128)} %get-tuple-element.108.r_7_, f32[4,4,16,128]{3,2,1,0:T(8,128)} %get-tuple-element.111, f32[4,6,32,128]{3,2,1,0:T(8,128)} %get-tuple-element.101, f32[4]{0:T(128)S(1)} %broadcast_multiply_fusion, f32[4]{0:T(128)S(1)} %broadcast_multiply_fusion.1, ...), kind=kLoop, calls=%fused_computation.8 | loop fusion | flops 229376 | bytes 461344 | tf_op jit(solution)/shard_map/convert_element_type | solution.py:461
  124.9 1.6 convert_element_type.66
  133.3 35.7 %shard_map.93 = f32[4,224,128]{2,1,0:T(8,128)} custom-call(bf16[2,2,4,224,128]{4,3,2,1,0:T(8,128)(2,1)} %pad.13.refs_0_, bf16[2,2,4,224,128]{4,3,2,1,0:T(8,128)(2,1)} %pad.14.refs_1_, bf16[2,2,4,224,128]{4,3,2,1,0:T(8,128)(2,1)} %pad.15.refs_2_, bf16[2,2,4,224,128]{4,3,2,1,0:T(8,128)(2,1)} %pad.16.refs_3_), custom_call_target="tpu_custom_call" | custom-call | tf_op jit(solution)/shard_map/pallas_call | solution.py:331
  169.1 1.0 slice.94
  170.2 1.0 copy.22
  (43 shorter events, 9.5 us)
Async XLA Ops:
  77.5 4.9 %copy-start.4 = (f32[16,8,128]{2,1,0:T(8,128)S(1)}, f32[16,8,128]{2,1,0:T(8,128)}, u32[]{:S(2)}) copy-start(f32[16,8,128]{2,1,0:T(8,128)} %get-tuple-element.88.r_2_) | copy-start | bytes 196612
  92.1 5.0 %copy-start.5 = (f32[16,8,128]{2,1,0:T(8,128)S(1)}, f32[16,8,128]{2,1,0:T(8,128)}, u32[]{:S(2)}) copy-start(f32[16,8,128]{2,1,0:T(8,128)} %get-tuple-element.96.r_2_) | copy-start | bytes 196612
  106.7 5.1 %copy-start.3 = (f32[16,8,128]{2,1,0:T(8,128)S(1)}, f32[16,8,128]{2,1,0:T(8,128)}, u32[]{:S(2)}) copy-start(f32[16,8,128]{2,1,0:T(8,128)} %get-tuple-element.107.r_2_) | copy-start | bytes 196612
  106.7 16.4 %copy-start.6 = (f32[4,128]{1,0:T(4,128)S(1)}, f32[4,128]{1,0:T(4,128)}, u32[]{:S(2)}) copy-start(f32[4,128]{1,0:T(4,128)} %get-tuple-element.102) | copy-start | bytes 6148
  126.4 1.8 %copy-start.2 = (f32[3456,128]{1,0:T(8,128)S(1)}, f32[3456,128]{1,0:T(8,128)}, u32[]{:S(2)}) copy-start(f32[3456,128]{1,0:T(8,128)} %get-tuple-element.116) | copy-start | bytes 5308420
  128.3 1.8 %copy-start.1 = (f32[3456,128]{1,0:T(8,128)S(1)}, f32[3456,128]{1,0:T(8,128)}, u32[]{:S(2)}) copy-start(f32[3456,128]{1,0:T(8,128)} %get-tuple-element.117) | copy-start | bytes 5308420
  130.2 1.8 %copy-start = (f32[3456,128]{1,0:T(8,128)S(1)}, f32[3456,128]{1,0:T(8,128)}, u32[]{:S(2)}) copy-start(f32[3456,128]{1,0:T(8,128)} %get-tuple-element.118) | copy-start | bytes 5308420
